TPU v7x, 128 devices: a whole 4x4x4 slice. The times are simulated.
128 devices in a mesh: row: 16 (over z, y_hi, core), col: 8 (over x, y_lo).
Axes of the slice: x: 4, y: 4 (y_hi: 2, y_lo: 2; y = y_hi * 2 + y_lo), z: 4, core: 2. Of those that a mesh axis runs over, the one named last changes fastest.
Arguments:
- inverse_tiles: bfloat16 [24576, 24576], P('row', 'col'), may hold values from -6 to 6
- factor: bfloat16 [24576, 2048], P('row', 'col'), may hold values from -0.0390625 to 0.0390625
- block_mask: int32 [192, 16], replicated, may hold values 0 or 1
- diag_inverse: float32 [16, 128, 128], replicated, may hold values from -6 to 6
Outputs:
- off_block: bfloat16 [2048, 24576], P('col', 'row')
- diag_block: float32 [16, 128, 128], P('col')
All inputs are finite; a program needn't handle non-finite values.
Results may differ from a plain program's by a relative error of at most 0.012.
Values may be sent and summed in bfloat16 or wider, within the bound.
A program may use at most 128 MiB of HBM per device.

v0:
```python
import jax
import jax.numpy as jnp
from jax import lax
from jax.sharding import Mesh
from jax.sharding import PartitionSpec as P

COL = ("col_0", "col_1")


def whole_of(x, axes, dim):
    for axis in reversed(axes):
        x = lax.all_gather(x, axis, axis=dim, tiled=True)
    return x


def filled_up(lines, length):
    spare = -lines.shape[0] % length
    if not spare:
        return lines
    return jnp.concatenate([lines, jnp.zeros((spare, *lines.shape[1:]), lines.dtype)])


def broadcast_by_parts(x, axis, root):
    lines = jnp.where(lax.axis_index(axis) == root, x, jnp.zeros_like(x)).reshape(
        -1, *x.shape[1:][-1:]
    )
    padded = filled_up(lines, lax.axis_size(axis))
    own = lax.psum_scatter(padded, axis, scatter_dimension=0, tiled=True)
    return lax.all_gather(own, axis, axis=0, tiled=True)[: len(lines)].reshape(x.shape)


def sum_by_axis(x, axes, dim):
    if not axes:
        return x
    nearer = lax.psum_scatter(x, axes[0], scatter_dimension=dim, tiled=True)
    return sum_by_axis(nearer, axes[1:], dim)


def sent_to_all(x, axis):
    length = lax.axis_size(axis)
    return lax.all_to_all(jnp.broadcast_to(x[None], (length, *x.shape)), axis, 0, 0, tiled=True)


def taken_together(x, axis):
    return sent_to_all(x, axis).astype(jnp.float32).sum(axis=0)


def per_device(inverse_tiles, factor, block_mask, diag_inverse):
    rows_here, cols_here = factor.shape
    block_width = diag_inverse.shape[1]
    sup_here = cols_here // block_width
    blocks_here = rows_here // block_width
    row_index = lax.axis_index("row")
    col_index = lax.axis_index(COL)
    mask_here = lax.dynamic_slice(
        block_mask, (row_index * blocks_here, col_index * sup_here), (blocks_here, sup_here)
    )
    keep_mask = jnp.repeat(jnp.repeat(mask_here, block_width, 0), block_width, 1).astype(
        jnp.bfloat16
    )
    masked = factor * keep_mask
    full_rows = whole_of(masked, COL, 1)
    row_ratio = lax.axis_size("row") // lax.axis_size(COL)
    row_pieces = []
    for offset in range(row_ratio):
        row_pieces.append(broadcast_by_parts(full_rows, "row", row_ratio * col_index + offset))
    summed = jnp.zeros((full_rows.shape[1], rows_here), jnp.float32)
    for offset in range(row_ratio):
        columns = row_pieces[offset]
        inverse_part = inverse_tiles[:, offset * rows_here : (offset + 1) * rows_here]
        summed = summed + lax.dot_general(
            columns, inverse_part, (((0,), (1,)), ((), ())), preferred_element_type=jnp.float32
        )
    reduced = sum_by_axis(summed, COL, 0)
    left_factor = masked.astype(jnp.float32).reshape(rows_here, sup_here, block_width)
    right_product = reduced.reshape(sup_here, block_width, rows_here)
    partial_diag = jnp.einsum(
        "jbr,rja->jab", right_product, left_factor, precision=lax.Precision.HIGHEST
    )
    summed_diag = taken_together(partial_diag.astype(jnp.bfloat16), "row").astype(jnp.float32)
    own_diag = lax.dynamic_slice_in_dim(diag_inverse, col_index * sup_here, sup_here, 0)
    return ((-reduced).astype(jnp.bfloat16), own_diag + summed_diag)


def solution(mesh):
    finer = Mesh(mesh.devices.reshape(mesh.shape["row"], 4, 2), ("row", "col_0", "col_1"))
    in_specs = (P("row", COL), P("row", COL), P(), P())
    out_specs = (P(COL, "row"), P(COL, None, None))
    return jax.shard_map(
        per_device, mesh=finer, in_specs=in_specs, out_specs=out_specs, check_vma=False
    )
```

profile of v0, /device:TPU:1, one launch (start us, length us, event | category | flops | bytes accessed | tf_op | source)
XLA Modules:
  0.0 650.2 jit_solution(2144273733660245835)
XLA Ops:
  7.2 0.0 all-gather.5.cloned.1.call-start
  7.2 0.8 dynamic-slice_convert_fusion
  8.0 0.1 copy.8
  8.1 0.1 broadcast_in_dim.12
  8.2 1.9 broadcast_in_dim.13
  10.1 2.1 bitcast_multiply_fusion
  12.3 0.0 all-gather.7.cloned.1.call-start
  12.3 33.0 %all-gather.5.cloned.1.call-done = bf16[1536,512]{1,0:T(8,128)(2,1)} async-done(((bf16[1536,256]{1,0:T(8,128)(2,1)}), bf16[1536,512]{1,0:T(8,128)(2,1)}) %all-gather.5.cloned.1.call-update) | async-done | bytes 1572880 | tf_op jit(solution)/shard_map/all_gather | solution.py:12
  45.3 0.0 reduce-scatter.5.cloned.1.call-start
  45.4 68.2 %all-gather.7.cloned.1.call-done = bf16[1536,2048]{1,0:T(8,128)(2,1)} async-done(((bf16[1536,512]{1,0:T(8,128)(2,1)}), bf16[1536,2048]{1,0:T(8,128)(2,1)}) %all-gather.7.cloned.1.call-update) | async-done | bytes 6291472 | tf_op jit(solution)/shard_map/all_gather | solution.py:12
  113.6 8.2 %broadcast_select_fusion = (bf16[1536,2048]{1,0:T(8,128)(2,1)}, bf16[1536,2048]{1,0:T(8,128)(2,1)}) fusion(bf16[1536,2048]{1,0:T(8,128)(2,1)} %all-gather.7.cloned.1.call-done, pred[]{:T(512)S(6)} %eq.7, pred[]{:T(512)S(6)} %eq.6), kind=kLoop, calls=%fused_computation.1 | loop fusion | flops 6291456 | bytes 18874370 | tf_op jit(solution)/shard_map/jit(_where)/select_n | solution.py:24
  121.8 0.0 reduce-scatter.7.cloned.1.call-start
  121.8 0.5 reduce-scatter.7.cloned.1.call-update
  122.4 0.0 all-gather.9.cloned.1.call-start
  122.4 88.9 %reduce-scatter.5.cloned.1.call-done = bf16[96,2048]{1,0:T(8,128)(2,1)} async-done(((bf16[1536,2048]{1,0:T(8,128)(2,1)}), bf16[96,2048]{1,0:T(8,128)(2,1)}) %reduce-scatter.5.cloned.1.call-update) | async-done | bytes 393232 | tf_op jit(solution)/shard_map/reduce_scatter | solution.py:28
  211.4 93.1 %reduce-scatter.7.cloned.1.call-done = bf16[96,2048]{1,0:T(8,128)(2,1)} async-done(((bf16[1536,2048]{1,0:T(8,128)(2,1)}), bf16[96,2048]{1,0:T(8,128)(2,1)}) %reduce-scatter.7.cloned.1.call-update) | async-done | bytes 393232 | tf_op jit(solution)/shard_map/reduce_scatter | solution.py:28
  304.6 0.0 reduce-scatter.9.cloned.1.call-start
  304.6 66.8 %all-gather.9.cloned.1.call-done = bf16[1536,2048]{1,0:T(8,128)(2,1)} async-done(((bf16[96,2048]{1,0:T(8,128)(2,1)}), bf16[1536,2048]{1,0:T(8,128)(2,1)}) %all-gather.9.cloned.1.call-update) | async-done | bytes 6291472 | tf_op jit(solution)/shard_map/all_gather | solution.py:29
  371.4 16.1 %fusion.1 = f32[2048,1536]{1,0:T(8,128)} fusion(bf16[1536,2048]{1,0:T(8,128)(2,1)} %all-gather.9.cloned.1.call-done, bf16[1536,3072]{1,0:T(8,128)(2,1)} %param.4), kind=kOutput, calls=%fused_computation.4 | convolution fusion | flops 9663676416 | bytes 23592960 | tf_op jit(solution)/shard_map/dot_general | solution.py:71
  387.5 48.2 %all-gather.11.cloned.1.call-done = bf16[1536,2048]{1,0:T(8,128)(2,1)} async-done(((bf16[96,2048]{1,0:T(8,128)(2,1)}), bf16[1536,2048]{1,0:T(8,128)(2,1)}) %all-gather.11.cloned.1.call-update) | async-done | bytes 6291472 | tf_op jit(solution)/shard_map/all_gather | solution.py:29
  435.7 17.9 %convolution_add_fusion = f32[2048,1536]{1,0:T(8,128)} fusion(f32[2048,1536]{1,0:T(8,128)} %fusion.1, bf16[1536,2048]{1,0:T(8,128)(2,1)} %all-gather.11.cloned.1.call-done, bf16[1536,3072]{1,0:T(8,128)(2,1)} %param.4), kind=kOutput, calls=%fused_computation | convolution fusion | flops 9666822144 | bytes 36175872 | tf_op jit(solution)/shard_map/dot_general | solution.py:71
  453.7 0.0 reduce-scatter.11.cloned.1.call-start
  453.7 111.8 %reduce-scatter.9.cloned.1.call-done = f32[512,1536]{1,0:T(8,128)} async-done(((f32[2048,1536]{1,0:T(8,128)}), f32[512,1536]{1,0:T(8,128)}) %reduce-scatter.9.cloned.1.call-update) | async-done | bytes 3145744 | tf_op jit(solution)/shard_map/reduce_scatter | solution.py:35
  565.6 0.3 copy.10
  565.9 47.6 %reduce-scatter.11.cloned.1.call-done = f32[256,1536]{1,0:T(8,128)} async-done(((f32[512,1536]{1,0:T(8,128)}), f32[256,1536]{1,0:T(8,128)}) %reduce-scatter.11.cloned.1.call-update) | async-done | bytes 1572880 | tf_op jit(solution)/shard_map/reduce_scatter | solution.py:35
  613.5 2.4 convolution_convert_fusion
  616.0 1.2 broadcast_in_dim.14
  617.2 7.3 %all-to-all-start = ((bf16[16,2,128,128]{3,2,1,0:T(8,128)(2,1)}), bf16[16,2,128,128]{3,2,1,0:T(8,128)(2,1)S(1)}, u32[]{:S(2)}, u32[]{:S(2)}) async-start(bf16[16,2,128,128]{3,2,1,0:T(8,128)(2,1)} %broadcast_in_dim.14), calls=%async_computation.4 | async-start | bytes 2097152 | tf_op jit(solution)/shard_map/all_to_all | solution.py:41
  624.5 1.0 negate_convert_fusion
  625.4 16.2 %all-to-all-done = bf16[16,2,128,128]{3,2,1,0:T(8,128)(2,1)S(1)} async-done(((bf16[16,2,128,128]{3,2,1,0:T(8,128)(2,1)}), bf16[16,2,128,128]{3,2,1,0:T(8,128)(2,1)S(1)}, u32[]{:S(2)}, u32[]{:S(2)}) %all-to-all-start) | async-done | bytes 1048608 | tf_op jit(solution)/shard_map/all_to_all | solution.py:41
  641.7 0.1 convert_reduce_fusion
  641.8 1.6 dynamic-slice_add_fusion
  (12 shorter events, 0.2 us)
Async XLA Ops:
  7.2 38.1 %all-gather.5.cloned.1.call-start = ((), (), s32[]{:S(2)}) async-start(), calls=%async_computation.5 | async-start | bytes 2359296 | tf_op jit(solution)/shard_map/all_gather | solution.py:12
  12.3 101.3 %all-gather.7.cloned.1.call-start = ((), (), s32[]{:S(2)}) async-start(), calls=%async_computation.6 | async-start | bytes 7864320 | tf_op jit(solution)/shard_map/all_gather | solution.py:12
  45.3 166.0 %reduce-scatter.5.cloned.1.call-start = ((), (), s32[]{:S(2)}) async-start(), calls=%async_computation.7 | async-start | bytes 6684672 | tf_op jit(solution)/shard_map/reduce_scatter | solution.py:28
  121.8 182.8 %reduce-scatter.7.cloned.1.call-start = ((), (), s32[]{:S(2)}) async-start(), calls=%async_computation.9 | async-start | bytes 6684672 | tf_op jit(solution)/shard_map/reduce_scatter | solution.py:28
  122.4 249.1 %all-gather.9.cloned.1.call-start = ((), (), s32[]{:S(2)}) async-start(), calls=%async_computation.8 | async-start | bytes 6684672 | tf_op jit(solution)/shard_map/all_gather | solution.py:29
  211.4 224.4 %all-gather.11.cloned.1.call-start = ((), (), s32[]{:S(2)}) async-start(), calls=%async_computation.10 | async-start | bytes 6684672 | tf_op jit(solution)/shard_map/all_gather | solution.py:29
  304.6 261.0 %reduce-scatter.9.cloned.1.call-start = ((), (), s32[]{:S(2)}) async-start(), calls=%async_computation.11 | async-start | bytes 15728640 | tf_op jit(solution)/shard_map/reduce_scatter | solution.py:35
  453.6 112.0 %copy-start = (bf16[1536,256]{1,0:T(8,128)(2,1)S(1)}, bf16[1536,256]{1,0:T(8,128)(2,1)}, u32[]{:S(2)}) copy-start(bf16[1536,256]{1,0:T(8,128)(2,1)} %bitcast_multiply_fusion) | copy-start | bytes 2359300
  453.7 159.8 %reduce-scatter.11.cloned.1.call-start = ((), (), s32[]{:S(2)}) async-start(), calls=%async_computation.12 | async-start | bytes 4718592 | tf_op jit(solution)/shard_map/reduce_scatter | solution.py:35
  613.5 10.9 %copy-start.1 = (f32[256,1536]{1,0:T(8,128)S(1)}, f32[256,1536]{1,0:T(8,128)}, u32[]{:S(2)}) copy-start(f32[256,1536]{1,0:T(8,128)} %reduce-scatter.11.cloned.1.call-done) | copy-start | bytes 4718596
  617.2 24.5 %all-to-all-start = ((bf16[16,2,128,128]{3,2,1,0:T(8,128)(2,1)}), bf16[16,2,128,128]{3,2,1,0:T(8,128)(2,1)S(1)}, u32[]{:S(2)}, u32[]{:S(2)}) async-start(bf16[16,2,128,128]{3,2,1,0:T(8,128)(2,1)} %broadcast_in_dim.14), calls=%async_computation.4 | async-start | bytes 2097152 | tf_op jit(solution)/shard_map/all_to_all | solution.py:41
Sparse Core Ops, SparseCore 0:
  12.4 32.8 all-gather.4
  47.0 66.5 all-gather.6
  121.9 89.3 reduce-scatter.4
  216.0 88.5 reduce-scatter.6
  306.8 64.5 all-gather.8
  373.8 61.9 all-gather.10
  453.8 111.7 reduce-scatter.8
  567.9 45.5 reduce-scatter.10
where the time goes:
time: 651 us; the launch traced here: 650 us
  waiting for transfers between devices  575 us (88%)
  matrix products  36.4 us (6%)
  between operations  14.2 us (2%)
  other arithmetic  13.8 us (2%)
  starting transfers between devices  7.6 us (1%)
    reduce_scatter x2, waiting for transfers between devices, broadcast_by_parts(): own = lax.psum_scatter(padded, axis, scatter_dimension=0, tiled=True)  182 us
    reduce_scatter x2, waiting for transfers between devices, sum_by_axis(): nearer = lax.psum_scatter(x, axes[0], scatter_dimension=dim, tiled=True)  159 us
    all_gather x2, waiting for transfers between devices, broadcast_by_parts(): lax.all_gather(own, axis, axis=0, tiled=True)[:len(lines)].reshape(x.shape)  115 us
    all_gather x2, waiting for transfers between devices, whole_of(): x = lax.all_gather(x, axis, axis=dim, tiled=True)  101 us
    dot_general x2, matrix products, per_device(): lax.dot_general(columns, inverse_part, (((0,), (1,)), ((), ())), preferre...  34 us
    all_to_all x1, waiting for transfers between devices, sent_to_all(): lax.all_to_all(jnp.broadcast_to(x[None], (length, *x.shape)), axis, 0, 0,...  16.2 us
  transfers between devices with their start and end apart: 9, of which 9 were waited for; matrix products, arithmetic and copies ran while one was open for 3% of the time, Pallas kernels for 0%

commit v1 on v0

--- a/solution.py
+++ b/solution.py
@@ -5,6 +5,15 @@
 from jax.sharding import PartitionSpec as P
 
 COL = ("col_0", "col_1")
+
+
+def measure_links_for(u, along_axis):
+    series = []
+    for _ in range(lax.axis_size(along_axis)):
+        series.append(u)
+    now = jnp.stack(series, 0)
+    all_rows = lax.all_to_all(now, along_axis, 0, 0)
+    return jnp.concatenate(all_rows, axis=0)
 
 
 def whole_of(x, axes, dim):
@@ -26,7 +35,7 @@
     )
     padded = filled_up(lines, lax.axis_size(axis))
     own = lax.psum_scatter(padded, axis, scatter_dimension=0, tiled=True)
-    return lax.all_gather(own, axis, axis=0, tiled=True)[: len(lines)].reshape(x.shape)
+    return measure_links_for(own, along_axis=axis)[: len(lines)].reshape(x.shape)
 
 
 def sum_by_axis(x, axes, dim):

time: 651 us -> 631 us (0.969)
  waiting for transfers between devices: 575 us -> 534 us
  starting transfers between devices: 7.6 us -> 20.1 us
  local copies, waits for them, and re-layouts: 3.59 us -> 12.5 us
    all_gather x2 -> x0, waiting for transfers between devices: 115 us -> none  [broadcast_by_parts(): lax.all_gather(own, axis, axis=0, tiled=True)[:len(lines)].reshape(x.shape)]
    all_to_all x0 -> x2, waiting for transfers between devices: none -> 57.3 us  [measure_links_for(): all_rows = lax.all_to_all(now, along_axis, 0, 0)]
    reduce_scatter x2, waiting for transfers between devices: 182 us -> 199 us  [broadcast_by_parts(): own = lax.psum_scatter(padded, axis, scatter_dimension=0, tiled=True)]
    all_to_all x0 -> x2, starting transfers between devices: none -> 12.4 us  [measure_links_for(): all_rows = lax.all_to_all(now, along_axis, 0, 0)]
    another operation x0 -> x2, local copies, waits for them, and re-layouts: none -> 8.91 us  [measure_links_for(): now = jnp.stack(series, 0)]
  transfers between devices with their start and end apart: 9 -> 9, of which waited for: 9 -> 8; matrix products, arithmetic and copies ran while one was open for 3% -> 3% of each run, Pallas kernels for 0% -> 0%
where the time goes in v1:
time: 631 us
  waiting for transfers between devices  534 us (85%)
  matrix products  36.5 us (6%)
  starting transfers between devices  20.1 us (3%)
  between operations  14.2 us (2%)
  other arithmetic  13.7 us (2%)
  local copies, waits for them, and re-layouts  12.5 us (2%)
    reduce_scatter x2, waiting for transfers between devices, broadcast_by_parts(): own = lax.psum_scatter(padded, axis, scatter_dimension=0, tiled=True)  199 us
    reduce_scatter x2, waiting for transfers between devices, sum_by_axis(): nearer = lax.psum_scatter(x, axes[0], scatter_dimension=dim, tiled=True)  160 us
    all_gather x2, waiting for transfers between devices, whole_of(): x = lax.all_gather(x, axis, axis=dim, tiled=True)  101 us
    all_to_all x2, waiting for transfers between devices, measure_links_for(): all_rows = lax.all_to_all(now, along_axis, 0, 0)  57.3 us
    dot_general x2, matrix products, per_device(): lax.dot_general(columns, inverse_part, (((0,), (1,)), ((), ())), preferre...  34.1 us
    all_to_all x1, waiting for transfers between devices, sent_to_all(): lax.all_to_all(jnp.broadcast_to(x[None], (length, *x.shape)), axis, 0, 0,...  16.2 us
  transfers between devices with their start and end apart: 9, of which 8 were waited for; matrix products, arithmetic and copies ran while one was open for 3% of the time, Pallas kernels for 0%

profile of v1, /device:TPU:1, one launch (start us, length us, event | category | flops | bytes accessed | tf_op | source)
XLA Modules:
  0.0 630.6 jit_solution(10231004914871061939)
XLA Ops:
  7.2 0.8 dynamic-slice_convert_fusion
  8.0 0.1 copy.8
  8.1 0.1 broadcast_in_dim.12
  8.2 1.9 broadcast_in_dim.13
  10.1 2.1 bitcast_multiply_fusion
  12.3 0.0 all-gather.5.cloned.1.call-start
  12.3 33.0 %all-gather.3.cloned.1.call-done = bf16[1536,512]{1,0:T(8,128)(2,1)} async-done(((bf16[1536,256]{1,0:T(8,128)(2,1)}), bf16[1536,512]{1,0:T(8,128)(2,1)}) %all-gather.3.cloned.1.call-update) | async-done | bytes 1572880 | tf_op jit(solution)/shard_map/all_gather | solution.py:21
  45.4 68.2 %all-gather.5.cloned.1.call-done = bf16[1536,2048]{1,0:T(8,128)(2,1)} async-done(((bf16[1536,512]{1,0:T(8,128)(2,1)}), bf16[1536,2048]{1,0:T(8,128)(2,1)}) %all-gather.5.cloned.1.call-update) | async-done | bytes 6291472 | tf_op jit(solution)/shard_map/all_gather | solution.py:21
  113.6 8.1 %broadcast_select_fusion = (bf16[1536,2048]{1,0:T(8,128)(2,1)}, bf16[1536,2048]{1,0:T(8,128)(2,1)}) fusion(bf16[1536,2048]{1,0:T(8,128)(2,1)} %all-gather.5.cloned.1.call-done, pred[]{:T(512)S(6)} %eq.7, pred[]{:T(512)S(6)} %eq.6), kind=kLoop, calls=%fused_computation.1 | loop fusion | flops 6291456 | bytes 18874370 | tf_op jit(solution)/shard_map/jit(_where)/select_n | solution.py:33
  121.7 0.0 reduce-scatter.7.cloned.1.call-start
  121.8 0.5 reduce-scatter.7.cloned.1.call-update
  122.3 89.0 %reduce-scatter.5.cloned.1.call-done = bf16[96,2048]{1,0:T(8,128)(2,1)} async-done(((bf16[1536,2048]{1,0:T(8,128)(2,1)}), bf16[96,2048]{1,0:T(8,128)(2,1)}) %reduce-scatter.5.cloned.1.call-update) | async-done | bytes 393232 | tf_op jit(solution)/shard_map/reduce_scatter | solution.py:37
  211.3 4.4 stack.4
  215.7 6.2 all-to-all-start
  221.9 109.6 %reduce-scatter.7.cloned.1.call-done = bf16[96,2048]{1,0:T(8,128)(2,1)} async-done(((bf16[1536,2048]{1,0:T(8,128)(2,1)}), bf16[96,2048]{1,0:T(8,128)(2,1)}) %reduce-scatter.7.cloned.1.call-update) | async-done | bytes 393232 | tf_op jit(solution)/shard_map/reduce_scatter | solution.py:37
  331.5 4.5 stack.5
  336.0 6.2 all-to-all-start.1
  342.2 0.2 reduce-scatter.9.cloned.1.call-start
  342.4 16.1 %fusion.1 = f32[2048,1536]{1,0:T(8,128)} fusion(bf16[1536,2048]{1,0:T(8,128)(2,1)} %bitcast.1, bf16[1536,3072]{1,0:T(8,128)(2,1)} %param.4), kind=kOutput, calls=%fused_computation.4 | convolution fusion | flops 9663676416 | bytes 23592960 | tf_op jit(solution)/shard_map/dot_general | solution.py:80
  358.5 57.3 %all-to-all-done.1 = bf16[16,96,2048]{2,1,0:T(8,128)(2,1)} async-done(((bf16[16,96,2048]{2,1,0:T(8,128)(2,1)}), bf16[16,96,2048]{2,1,0:T(8,128)(2,1)}, u32[]{:S(2)}, u32[]{:S(2)}) %all-to-all-start.1) | async-done | bytes 6291488 | tf_op jit(solution)/shard_map/all_to_all | solution.py:15
  415.8 17.9 %convolution_add_fusion = f32[2048,1536]{1,0:T(8,128)} fusion(f32[2048,1536]{1,0:T(8,128)} %fusion.1, bf16[1536,2048]{1,0:T(8,128)(2,1)} %bitcast.2, bf16[1536,3072]{1,0:T(8,128)(2,1)} %param.4), kind=kOutput, calls=%fused_computation | convolution fusion | flops 9666822144 | bytes 36175872 | tf_op jit(solution)/shard_map/dot_general | solution.py:80
  433.8 0.0 reduce-scatter.11.cloned.1.call-start
  433.8 112.3 %reduce-scatter.9.cloned.1.call-done = f32[512,1536]{1,0:T(8,128)} async-done(((f32[2048,1536]{1,0:T(8,128)}), f32[512,1536]{1,0:T(8,128)}) %reduce-scatter.9.cloned.1.call-update) | async-done | bytes 3145744 | tf_op jit(solution)/shard_map/reduce_scatter | solution.py:44
  546.2 0.3 copy.10
  546.4 47.5 %reduce-scatter.11.cloned.1.call-done = f32[256,1536]{1,0:T(8,128)} async-done(((f32[512,1536]{1,0:T(8,128)}), f32[256,1536]{1,0:T(8,128)}) %reduce-scatter.11.cloned.1.call-update) | async-done | bytes 1572880 | tf_op jit(solution)/shard_map/reduce_scatter | solution.py:44
  593.9 2.4 convolution_convert_fusion
  596.4 1.2 broadcast_in_dim.14
  597.6 7.3 %all-to-all-start.2 = ((bf16[16,2,128,128]{3,2,1,0:T(8,128)(2,1)}), bf16[16,2,128,128]{3,2,1,0:T(8,128)(2,1)S(1)}, u32[]{:S(2)}, u32[]{:S(2)}) async-start(bf16[16,2,128,128]{3,2,1,0:T(8,128)(2,1)} %broadcast_in_dim.14), calls=%async_computation.6 | async-start | bytes 2097152 | tf_op jit(solution)/shard_map/all_to_all | solution.py:50
  604.9 1.0 negate_convert_fusion
  605.8 16.2 %all-to-all-done.2 = bf16[16,2,128,128]{3,2,1,0:T(8,128)(2,1)S(1)} async-done(((bf16[16,2,128,128]{3,2,1,0:T(8,128)(2,1)}), bf16[16,2,128,128]{3,2,1,0:T(8,128)(2,1)S(1)}, u32[]{:S(2)}, u32[]{:S(2)}) %all-to-all-start.2) | async-done | bytes 1048608 | tf_op jit(solution)/shard_map/all_to_all | solution.py:50
  622.1 0.1 convert_reduce_fusion
  622.2 1.6 dynamic-slice_add_fusion
  (12 shorter events, 0.2 us)
Async XLA Ops:
  7.2 38.1 %all-gather.3.cloned.1.call-start = ((), (), s32[]{:S(2)}) async-start(), calls=%async_computation.7 | async-start | bytes 2359296 | tf_op jit(solution)/shard_map/all_gather | solution.py:21
  12.3 101.3 %all-gather.5.cloned.1.call-start = ((), (), s32[]{:S(2)}) async-start(), calls=%async_computation.8 | async-start | bytes 7864320 | tf_op jit(solution)/shard_map/all_gather | solution.py:21
  45.3 166.0 %reduce-scatter.5.cloned.1.call-start = ((), (), s32[]{:S(2)}) async-start(), calls=%async_computation.9 | async-start | bytes 6684672 | tf_op jit(solution)/shard_map/reduce_scatter | solution.py:37
  121.7 209.7 %reduce-scatter.7.cloned.1.call-start = ((), (), s32[]{:S(2)}) async-start(), calls=%async_computation.10 | async-start | bytes 6684672 | tf_op jit(solution)/shard_map/reduce_scatter | solution.py:37
  215.7 115.7 %all-to-all-start = ((bf16[16,96,2048]{2,1,0:T(8,128)(2,1)}), bf16[16,96,2048]{2,1,0:T(8,128)(2,1)}, u32[]{:S(2)}, u32[]{:S(2)}) async-start(bf16[16,96,2048]{2,1,0:T(8,128)(2,1)} %stack.4), calls=%async_computation.1 | async-start | bytes 12582912 | tf_op jit(solution)/shard_map/all_to_all | solution.py:15
  336.0 79.9 %all-to-all-start.1 = ((bf16[16,96,2048]{2,1,0:T(8,128)(2,1)}), bf16[16,96,2048]{2,1,0:T(8,128)(2,1)}, u32[]{:S(2)}, u32[]{:S(2)}) async-start(bf16[16,96,2048]{2,1,0:T(8,128)(2,1)} %stack.5), calls=%async_computation.3 | async-start | bytes 12582912 | tf_op jit(solution)/shard_map/all_to_all | solution.py:15
  342.2 203.9 %reduce-scatter.9.cloned.1.call-start = ((), (), s32[]{:S(2)}) async-start(), calls=%async_computation.11 | async-start | bytes 15728640 | tf_op jit(solution)/shard_map/reduce_scatter | solution.py:44
  433.7 112.4 %copy-start = (bf16[1536,256]{1,0:T(8,128)(2,1)S(1)}, bf16[1536,256]{1,0:T(8,128)(2,1)}, u32[]{:S(2)}) copy-start(bf16[1536,256]{1,0:T(8,128)(2,1)} %bitcast_multiply_fusion) | copy-start | bytes 2359300
  433.8 160.1 %reduce-scatter.11.cloned.1.call-start = ((), (), s32[]{:S(2)}) async-start(), calls=%async_computation.12 | async-start | bytes 4718592 | tf_op jit(solution)/shard_map/reduce_scatter | solution.py:44
  593.9 10.9 %copy-start.1 = (f32[256,1536]{1,0:T(8,128)S(1)}, f32[256,1536]{1,0:T(8,128)}, u32[]{:S(2)}) copy-start(f32[256,1536]{1,0:T(8,128)} %reduce-scatter.11.cloned.1.call-done) | copy-start | bytes 4718596
  597.6 24.5 %all-to-all-start.2 = ((bf16[16,2,128,128]{3,2,1,0:T(8,128)(2,1)}), bf16[16,2,128,128]{3,2,1,0:T(8,128)(2,1)S(1)}, u32[]{:S(2)}, u32[]{:S(2)}) async-start(bf16[16,2,128,128]{3,2,1,0:T(8,128)(2,1)} %broadcast_in_dim.14), calls=%async_computation.6 | async-start | bytes 2097152 | tf_op jit(solution)/shard_map/all_to_all | solution.py:50
Sparse Core Ops, SparseCore 0:
  12.4 32.8 all-gather.2
  47.0 66.5 all-gather.4
  121.9 89.3 reduce-scatter.4
  215.9 115.5 reduce-scatter.6
  433.9 112.1 reduce-scatter.8
  548.3 45.5 reduce-scatter.10
